TPU v7x, 32 devices: a whole 2x2x4 slice. The times are simulated.
32 devices in a mesh: groups: 2 (over x), tp: 16 (over z, y, core).
Axes of the slice: x: 2, y: 2, z: 4, core: 2. Of those that a mesh axis runs over, the one named last changes fastest.
Arguments:
- tokens: bfloat16 [256, 8192], P(('groups', 'tp')), parts along dimension 0, may hold values from -6 to 6
- gate_blocks: bfloat16 [128, 32, 128, 128], P('tp'), may hold values from -0.09375 to 0.09375
- gate_rows: int32 [128, 32], P('tp'), may hold values from 0 to 63, as said below
- up_blocks: bfloat16 [128, 32, 128, 128], P('tp'), may hold values from -0.09375 to 0.09375
- up_rows: int32 [128, 32], P('tp'), may hold values from 0 to 63, as said below
- down_blocks: bfloat16 [128, 32, 128, 128], P('tp'), may hold values from -0.0625 to 0.0625
- down_cols: int32 [128, 32], P('tp'), may hold values from 0 to 63, as said below
- owner: int32 [64], P('tp'), may hold values from 0 to 63, each once
Outputs:
- mixed_blocks: bfloat16 [64, 256, 128], P('tp', 'groups'), parts along dimension 1
There are 2 independent parts, one for each index of `groups`. A program takes and returns all parts, laid end to end along the dimension named above; an argument that names none is the same for every part. Nothing has to cross between parts.
Inputs may be any that keep to these rules, and one draw needn't show every extreme that they name: `gate_rows`: each row lists 32 distinct row blocks in increasing order. `up_rows`: each row lists 32 distinct row blocks in increasing order. `down_cols`: each row lists 32 distinct output blocks in increasing order; rows 2g and 2g+1 list disjoint blocks, together all 64.
All inputs are finite; a program needn't handle non-finite values.
Results may differ from a plain program's by a relative error of at most 0.0049.
Values may be sent and summed in bfloat16 or wider, within the bound.
A program may use at most 192 MiB of HBM per device.

v0:
```python
import jax
import jax.numpy as jnp
from jax import lax
from jax.sharding import PartitionSpec as P


def fill_dense(blocks, rows_list, width_blocks):
    onehot = (
        rows_list[:, :, None] == jnp.arange(width_blocks, dtype=jnp.int32)[None, None, :]
    ).astype(jnp.bfloat16)
    dense = jnp.einsum("jkd,jkcf->dcjf", onehot, blocks, preferred_element_type=jnp.float32)
    return dense.astype(jnp.bfloat16).reshape(
        width_blocks * blocks.shape[2], blocks.shape[0] * blocks.shape[3]
    )


def body(tokens, gate_blocks, gate_rows, up_blocks, up_rows, down_blocks, down_cols, owner):
    blk = gate_blocks.shape[2]
    local_hidden = gate_blocks.shape[0]
    width_blocks = tokens.shape[1] // blk
    dense_gate = fill_dense(gate_blocks, gate_rows, width_blocks)
    dense_up = fill_dense(up_blocks, up_rows, width_blocks)
    piece = lax.all_gather(tokens, "tp", axis=0, tiled=True)
    nrows = piece.shape[0]
    gate = jnp.dot(piece, dense_gate, preferred_element_type=jnp.float32).reshape(
        nrows, local_hidden, blk
    )
    up = jnp.dot(piece, dense_up, preferred_element_type=jnp.float32).reshape(
        nrows, local_hidden, blk
    )
    hidden = (jax.nn.silu(gate) * up).astype(jnp.bfloat16)
    ntok = hidden.shape[0]
    owners_all = lax.all_gather(owner, "tp", axis=0, tiled=True)
    slot_onehot = (down_cols[:, :, None] == owners_all[None, None, :]).astype(jnp.bfloat16)
    dense_down = jnp.einsum(
        "jks,jkfc->sjfc", slot_onehot, down_blocks, preferred_element_type=jnp.float32
    )
    dense_down = dense_down.astype(jnp.bfloat16).reshape(width_blocks, local_hidden * blk, blk)
    hidden_flat = hidden.reshape(ntok, local_hidden * blk)
    summed = lax.psum_scatter(
        jnp.einsum("tf,sfc->stc", hidden_flat, dense_down, preferred_element_type=jnp.float32),
        "tp",
        scatter_dimension=0,
        tiled=True,
    )
    return summed.astype(jnp.bfloat16)


def solution(mesh):
    in_specs = (
        P(("groups", "tp"), None),
        P("tp", None, None, None),
        P("tp", None),
        P("tp", None, None, None),
        P("tp", None),
        P("tp", None, None, None),
        P("tp", None),
        P("tp"),
    )
    out_specs = P("tp", "groups", None)
    return jax.shard_map(body, mesh=mesh, in_specs=in_specs, out_specs=out_specs, check_vma=False)
```

profile of v0, /device:TPU:0, one launch (start us, length us, event | category | flops | bytes accessed | tf_op | source)
XLA Modules:
  0.0 233.0 jit_solution(15418638487142140796)
XLA Ops:
  6.5 0.0 all-gather.2.cloned.1.call-start
  6.5 0.7 all-gather.2.cloned.1.call-update
  7.3 0.0 reduce-scatter.2.cloned.1.call-start
  7.3 0.0 slice-start
  7.3 14.9 %convert_bitcast_fusion.1 = bf16[64,128,8,128]{3,0,1,2:T(8,128)(2,1)} fusion(bf16[8,32,128,128]{3,2,1,0:T(8,128)(2,1)} %param.9, s32[8,32]{1,0:T(8,128)} %param.10), kind=kOutput, calls=%fused_computation.9 | convolution fusion | flops 545275904 | bytes 25166848 | tf_op jit(solution)/shard_map/jkd,jkcf->dcjf/dot_general | solution.py:11
  22.2 0.0 slice-start.1
  22.3 0.0 copy-start
  22.3 18.8 %copy.16 = bf16[64,128,8,128]{3,2,1,0:T(8,128)(2,1)} copy(bf16[64,128,8,128]{3,0,1,2:T(8,128)(2,1)} %convert_bitcast_fusion.1) | data formatting | bytes 33554432 | tf_op jit(solution)/shard_map/convert_element_type | solution.py:12
  41.1 0.0 slice-done
  41.1 0.0 slice-done.1
  41.1 0.0 copy-done
  41.1 9.2 %convert_bitcast_fusion = bf16[64,128,8,128]{3,0,1,2:T(8,128)(2,1)} fusion(bf16[8,32,128,128]{3,2,1,0:T(8,128)(2,1)S(1)} %bitcast.54, s32[8,32]{1,0:T(8,128)S(1)} %copy-done), kind=kOutput, calls=%fused_computation.8 | convolution fusion | flops 545275904 | bytes 25166848 | tf_op jit(solution)/shard_map/jkd,jkcf->dcjf/dot_general | solution.py:11
  50.2 0.0 copy-start.3
  50.2 0.0 copy-start.2
  50.2 0.0 copy-start.1
  50.2 18.6 %copy.20 = bf16[64,128,8,128]{3,2,1,0:T(8,128)(2,1)} copy(bf16[64,128,8,128]{3,0,1,2:T(8,128)(2,1)} %convert_bitcast_fusion) | data formatting | bytes 33554432 | tf_op jit(solution)/shard_map/convert_element_type | solution.py:12
  68.8 0.0 copy-done.3
  68.8 0.6 dynamic-slice
  70.1 0.0 copy-done.2
  70.1 0.2 dynamic-update-slice
  70.3 13.6 %all-reduce = s32[64]{0:T(128)S(1)} all-reduce(s32[64]{0:T(128)S(1)} %dynamic-update-slice), channel_id=1, replica_groups=mesh['groups'=2,'tp'=16] {'tp'}, use_global_device_ids=true, to_apply=%add | all-reduce | flops 64 | bytes 512
  83.9 0.0 copy-done.1
  83.9 14.8 %fusion.9 = bf16[8,64,128,128]{3,1,2,0:T(8,128)(2,1)} fusion(bf16[8,32,128,128]{3,2,1,0:T(8,128)(2,1)} %param.13, s32[64]{0:T(128)S(1)} %all-reduce, s32[8,32]{1,0:T(8,128)S(1)} %copy-done.1), kind=kOutput, calls=%fused_computation.11 | convolution fusion | flops 536887296 | bytes 25167104 | tf_op jit(solution)/shard_map/jks,jkfc->sjfc/dot_general | solution.py:35
  98.7 23.0 %copy.25 = bf16[8,64,128,128]{2,3,0,1:T(8,128)(2,1)} copy(bf16[8,64,128,128]{3,1,2,0:T(8,128)(2,1)} %fusion.9) | data formatting | bytes 33554432 | tf_op jit(solution)/shard_map/jks,jkfc->sjfc/dot_general | solution.py:35
  121.7 0.0 all-gather.2.cloned.1.call-done
  121.7 10.9 %fusion.3 = f32[1024,128]{1,0:T(8,128)S(1)} fusion(bf16[128,8192]{1,0:T(8,128)(2,1)} %all-gather.2.cloned.1.call-done, bf16[1024,8,8,128]{3,2,1,0:T(8,128)(2,1)} %bitcast.52), kind=kOutput, calls=%fused_computation.3 | convolution fusion | flops 2147483648 | bytes 19398656 | tf_op jit(solution)/shard_map/dot_general | solution.py:25
  132.6 0.2 copy.18
  132.8 10.9 %fusion = f32[1024,128]{1,0:T(8,128)S(1)} fusion(bf16[128,8192]{1,0:T(8,128)(2,1)} %all-gather.2.cloned.1.call-done, bf16[1024,8,8,128]{3,2,1,0:T(8,128)(2,1)} %bitcast.51), kind=kOutput, calls=%fused_computation | convolution fusion | flops 2147483648 | bytes 19398656 | tf_op jit(solution)/shard_map/dot_general | solution.py:28
  143.8 0.2 copy.21
  144.0 10.4 %fusion.13 = f32[64,128,128]{1,2,0:T(8,128)} fusion(bf16[8,64,128,128]{2,3,0,1:T(8,128)(2,1)} %copy.25, f32[128,8,128]{2,0,1:T(8,128)S(1)} %copy.21, f32[128,8,128]{2,0,1:T(8,128)S(1)} %copy.18), kind=kOutput, calls=%fused_computation.15 | convolution fusion | flops 2148270080 | bytes 22020096 | tf_op jit(solution)/shard_map/tf,sfc->stc/dot_general | solution.py:41
  154.3 0.0 reduce-scatter.2.cloned.1.call-update
  154.4 70.0 %reduce-scatter.2.cloned.1.call-done = f32[4,128,128]{1,2,0:T(8,128)} async-done(((f32[64,128,128]{1,2,0:T(8,128)}), f32[4,128,128]{1,2,0:T(8,128)}) %reduce-scatter.2.cloned.1.call-update) | async-done | bytes 262160 | tf_op jit(solution)/shard_map/reduce_scatter | solution.py:40
  224.4 1.0 convert_element_type.34
  225.3 0.8 copy.22
  (2 shorter events, 0.0 us)
Async XLA Ops:
  6.5 115.2 %all-gather.2.cloned.1.call-start = ((), (), s32[]{:S(2)}) async-start(), calls=%async_computation.1 | async-start | bytes 2228224 | tf_op jit(solution)/shard_map/all_gather | solution.py:23
  7.3 217.1 %reduce-scatter.2.cloned.1.call-start = ((), (), s32[]{:S(2)}) async-start(), calls=%async_computation.2 | async-start | bytes 4456448 | tf_op jit(solution)/shard_map/reduce_scatter | solution.py:40
  7.3 33.8 %slice-start = ((s8[8388608]{0:T(1024)(128)(4,1)}), s8[4194304]{0:T(1024)(128)(4,1)S(1)}, s32[]{:S(2)}) async-start(s8[8388608]{0:T(1024)(128)(4,1)} %bitcast.53), calls=%async_computation.3 | async-start | bytes 8388608
  22.2 18.8 %slice-start.1 = ((s8[8388608]{0:T(1024)(128)(4,1)}), s8[4194304]{0:T(1024)(128)(4,1)S(1)}, s32[]{:S(2)}) async-start(s8[8388608]{0:T(1024)(128)(4,1)} %bitcast.53), calls=%async_computation.4 | async-start | bytes 8388608
  22.3 18.8 %copy-start = (s32[8,32]{1,0:T(8,128)S(1)}, s32[8,32]{1,0:T(8,128)}, u32[]{:S(2)}) copy-start(s32[8,32]{1,0:T(8,128)} %param.12) | copy-start | bytes 3076
  50.2 18.6 %copy-start.3 = (u32[32]{0:T(128)S(1)}, u32[32]{0:T(128)}, u32[]{:S(2)}) copy-start(u32[32]{0:T(128)} %constant.13) | copy-start | bytes 388
  50.2 19.8 %copy-start.2 = (s32[4]{0:T(128)S(1)}, s32[4]{0:T(128)}, u32[]{:S(2)}) copy-start(s32[4]{0:T(128)} %param.15) | copy-start | bytes 52
  50.2 33.7 %copy-start.1 = (s32[8,32]{1,0:T(8,128)S(1)}, s32[8,32]{1,0:T(8,128)}, u32[]{:S(2)}) copy-start(s32[8,32]{1,0:T(8,128)} %param.14) | copy-start | bytes 3076
Sparse Core Ops, SparseCore 0:
  9.5 44.0 all-gather.1
  154.5 69.8 reduce-scatter.1
where the time goes:
time: 234 us; the launch traced here: 233 us
  matrix products  71.1 us (30%)
  waiting for transfers between devices  70.7 us (30%)
  local copies, waits for them, and re-layouts  62.4 us (27%)
  between operations  14.1 us (6%)
  blocking collectives  13.6 us (6%)
    reduce_scatter x1, waiting for transfers between devices, body(): lax.psum_scatter(jnp.einsum('tf,sfc->stc', hidden_flat, dense_down, prefe...  70 us
    convert_element_type x2, local copies, waits for them, and re-layouts, fill_dense(): dense.astype(jnp.bfloat16)  37.4 us
    dot_general x2, matrix products, fill_dense(): jnp.einsum('jkd,jkcf->dcjf', onehot, blocks, preferred_element_type=jnp.f...  24.1 us
    dot_general x1, local copies, waits for them, and re-layouts, body(): jnp.einsum('jks,jkfc->sjfc', slot_onehot, down_blocks, preferred_element_...  23 us
    dot_general x1, matrix products, body(): jnp.einsum('jks,jkfc->sjfc', slot_onehot, down_blocks, preferred_element_...  14.8 us
    unnamed x1, blocking collectives  13.6 us
    dot_general x1, matrix products, body(): jnp.dot(piece, dense_up, preferred_element_type=jnp.float32)  10.9 us
    dot_general x1, matrix products, body(): jnp.dot(piece, dense_gate, preferred_element_type=jnp.float32)  10.9 us
  transfers between devices with their start and end apart: 2, of which 1 were waited for; matrix products, arithmetic and copies ran while one was open for 43% of the time, Pallas kernels for 0%

commit v1 on v0

v1 whole, which is shorter than its diff:
```python
import functools

import jax
import jax.numpy as jnp
from jax import lax
from jax.experimental import pallas as pl
from jax.experimental.pallas import tpu as pltpu
from jax.sharding import PartitionSpec as P

MESH = pl.DeviceIdType.MESH
BF = jnp.bfloat16
F32 = jnp.float32


def kernel(
    nz, ny,
    tok_ref, grows, urows, dcols, own_ref, wg_hbm, wu_hbm, wd_hbm,
    out_ref,
    wg, wu, wd, buf, xs, hid, inv_v, inv_s, own_v, own_s,
    sib_out, sib_in, y_out, y_in, z_out, zup_in, zdn_in, fin,
    wsem, wdsem, tsem, tok_send, tok_recv,
    sib_s, sib_r, ys_s, ys_r, z_s, zup_r, zdn_r,
):
    n = nz * ny * 2
    hbl, keep, blk = wg.shape[0], wg.shape[1], wg.shape[2]
    pairs = hbl // 2
    half = tok_ref.shape[1] // (2 * blk)
    rows = tok_ref.shape[0]
    ntok = rows * n
    sp = out_ref.shape[0]

    me = lax.axis_index("tp")
    c = me % 2
    y = (me // 2) % ny
    z = me // (2 * ny)

    def at(z_, y_, c_):
        return (z_ * ny + y_) * 2 + c_

    sib = at(z, y, 1 - c)
    ynb = at(z, 1 - y, c) if ny == 2 else me
    zup = at(z + 1, y, c)
    zdn = at(z - 1, y, c)
    has_up = z + 1 < nz
    has_dn = z > 0

    def wcopy(i, j):
        src, dst = ((wg_hbm, wg), (wu_hbm, wu))[i]
        return pltpu.make_async_copy(src.at[j], dst.at[j], wsem.at[i, j])

    down_copy = pltpu.make_async_copy(wd_hbm, wd, wdsem)

    for g in range(half):
        lo = tok_ref[:, 2 * g * blk:(2 * g + 1) * blk].astype(F32)
        hi = tok_ref[:, (2 * g + 1) * blk:(2 * g + 2) * blk].astype(F32)
        buf[me, g] = jnp.concatenate([lo, hi], axis=0).astype(BF)
    lane = lax.broadcasted_iota(jnp.int32, (2 * rows, blk), 1)
    mine = jnp.zeros((2 * rows, blk), jnp.int32)
    for i in range(sp):
        mine = jnp.where(lane == me * sp + i, own_ref[i], mine)
    buf[me, half] = mine.astype(F32).astype(BF)

    barrier = pltpu.get_barrier_semaphore()

    def hello(dev):
        pl.semaphore_signal(barrier, inc=1, device_id={"tp": dev}, device_id_type=MESH)

    hello(sib)
    if ny == 2:
        hello(ynb)

    @pl.when(has_up)
    def _():
        hello(zup)

    @pl.when(has_dn)
    def _():
        hello(zdn)

    pl.semaphore_wait(barrier, ny + has_up.astype(jnp.int32) + has_dn.astype(jnp.int32))

    def tcopy(kind, slot):
        dev = (zup, zdn, ynb, sib)[kind]
        return pltpu.make_async_remote_copy(
            src_ref=buf.at[slot], dst_ref=buf.at[slot],
            send_sem=tok_send.at[kind, slot], recv_sem=tok_recv.at[slot],
            device_id={"tp": dev}, device_id_type=MESH)

    def arrived(slot):
        tcopy(3, slot).wait_recv()

    @pl.when(has_up)
    def _():
        tcopy(0, me).start()

    @pl.when(has_dn)
    def _():
        tcopy(1, me).start()

    if ny == 2:
        tcopy(2, me).start()
    tcopy(3, me).start()

    def start_w(j, _):
        wcopy(0, j).start()
        wcopy(1, j).start()
        return 0

    lax.fori_loop(0, hbl, start_w, 0)
    down_copy.start()

    row_id = lax.broadcasted_iota(jnp.int32, (8, blk), 0)
    lane8 = lax.broadcasted_iota(jnp.int32, (8, blk), 1)
    inv = jnp.zeros((8, blk), jnp.int32)

    def inv_step(k, acc):
        for j in range(hbl):
            hit = jnp.logical_and(lane8 == dcols[j, k], row_id == j // 2)
            acc = jnp.where(hit, (j % 2) * keep + k, acc)
        return acc

    inv_v[...] = lax.fori_loop(0, keep, inv_step, inv)
    inv_copy = pltpu.make_async_copy(inv_v, inv_s, tsem.at[0])
    inv_copy.start()

    def relayout(z_, y_):
        s0 = at(z_, y_, 0)
        chip = z_ * ny + y_

        def step(g, _):
            a = buf[s0, g].astype(F32)
            b = buf[s0 + 1, g].astype(F32)
            xs[2 * g, chip] = jnp.concatenate([a[:rows], b[:rows]], axis=0).astype(BF)
            xs[2 * g + 1, chip] = jnp.concatenate([a[rows:], b[rows:]], axis=0).astype(BF)
            return 0

        lax.fori_loop(0, half, step, 0, unroll=8)

    def sides(d, fn):
        @pl.when(z - d >= 0)
        def _():
            fn(z - d, 0)

        @pl.when(z + d < nz)
        def _():
            fn(z + d, 1)

    def zline(z_, from_up):
        slot = at(z_, y, c)
        arrived(slot)
        if from_up:
            @pl.when(has_dn)
            def _():
                tcopy(1, slot).start()
        else:
            @pl.when(has_up)
            def _():
                tcopy(0, slot).start()
        if ny == 2:
            tcopy(2, slot).start()
        tcopy(3, slot).start()

    def yline(z_, _):
        slot = at(z_, 1 - y, c)
        arrived(slot)
        tcopy(3, slot).start()

    def own_line(z_, _):
        arrived(at(z_, y, 1 - c))
        relayout(z_, y)

    def other_line(z_, _):
        arrived(at(z_, 1 - y, 1 - c))
        relayout(z_, 1 - y)

    def gather_step(d, _):
        sides(d, zline)

        @pl.when(d == 1)
        def _():
            if ny == 2:
                yline(z, 0)
            own_line(z, 0)

        @pl.when(d > 1)
        def _():
            if ny == 2:
                sides(d - 1, yline)
            sides(d - 1, own_line)
        return 0

    lax.fori_loop(1, nz, gather_step, 0)
    sides(nz - 1, own_line)
    if ny == 2:
        other_line(z, 0)

        def other_step(d, _):
            @pl.when(d < nz - 1)
            def _():
                sides(d, other_line)
            return 0

        lax.fori_loop(1, nz, other_step, 0)
        sides(nz - 1, yline)
        sides(nz - 1, other_line)

    own_row = buf[0, half].astype(F32)
    for s in range(1, n):
        own_row = own_row + buf[s, half].astype(F32)
    own_v[...] = own_row[:8].astype(jnp.int32)
    own_copy = pltpu.make_async_copy(own_v, own_s, tsem.at[1])
    own_copy.start()

    step_k = 8 if keep % 8 == 0 else keep

    def project(w, idx, j):
        acc = None
        for k in range(0, keep, step_k):
            lhs = jnp.concatenate(
                [xs[idx[j, k + i]].reshape(ntok, blk) for i in range(step_k)], axis=1)
            rhs = w[j, k:k + step_k].reshape(step_k * blk, blk)
            part = jnp.dot(lhs, rhs, preferred_element_type=F32)
            acc = part if acc is None else acc + part
        return acc

    def hidden_step(j, _):
        wcopy(0, j).wait()
        wcopy(1, j).wait()
        gate = project(wg, grows, j)
        up = project(wu, urows, j)
        hid[j] = (gate / (1.0 + jnp.exp(-gate)) * up).astype(BF)
        return 0

    lax.fori_loop(0, hbl, hidden_step, 0)

    inv_copy.wait()
    own_copy.wait()
    down_copy.wait()

    def term(dev, i):
        col = jnp.clip(own_s[0, dev * sp + i], 0, 2 * half - 1)
        lhs, rhs = [], []
        for p in range(pairs):
            q = inv_s[p, col]
            lhs.append(hid[2 * p + q // keep])
            rhs.append(wd[2 * p + q // keep, q % keep])
        return jnp.dot(jnp.concatenate(lhs, axis=1), jnp.concatenate(rhs, axis=0),
                       preferred_element_type=F32)

    above = nz - 1 - z
    far = jnp.maximum(z, above)
    near = jnp.minimum(z, above)
    sign = jnp.where(above >= z, 1, -1)

    def target(t):
        u = t - (far - near)
        first = u < 0
        dist = jnp.where(first, far - t, near - u // 2)
        side = jnp.where(jnp.logical_or(first, u % 2 == 0), sign, -sign)
        return z + jnp.where(t == nz - 1, 0, side * dist)

    def scopy(k, t):
        return pltpu.make_async_remote_copy(
            src_ref=sib_out.at[k, t], dst_ref=sib_in.at[k, t],
            send_sem=sib_s.at[k, t], recv_sem=sib_r.at[k, t],
            device_id={"tp": sib}, device_id_type=MESH)

    def ycopy(t):
        return pltpu.make_async_remote_copy(
            src_ref=y_out.at[t], dst_ref=y_in.at[t],
            send_sem=ys_s.at[t], recv_sem=ys_r.at[t],
            device_id={"tp": ynb}, device_id_type=MESH)

    def zcopy(upward, t):
        return pltpu.make_async_remote_copy(
            src_ref=z_out.at[t], dst_ref=(zup_in if upward else zdn_in).at[t],
            send_sem=z_s.at[t], recv_sem=(zup_r if upward else zdn_r).at[t],
            device_id={"tp": zup if upward else zdn}, device_id_type=MESH)

    def to_sibling(k, y_):
        def step(t, _):
            t = target(t)
            for i in range(sp):
                sib_out[k, t, i] = term(at(t, y_, 1 - c), i).astype(BF)
            scopy(k, t).start()
            return 0

        lax.fori_loop(0, nz, step, 0)

    if ny == 2:
        to_sibling(0, 1 - y)

        def to_y(t, _):
            t = target(t)
            scopy(0, t).wait_recv()
            for i in range(sp):
                y_out[t, i] = (term(at(t, 1 - y, c), i) + sib_in[0, t, i].astype(F32)).astype(BF)
            ycopy(t).start()
            return 0

        lax.fori_loop(0, nz, to_y, 0)

    to_sibling(1, y)

    def to_z(t, _):
        t = target(t)
        scopy(1, t).wait_recv()
        if ny == 2:
            ycopy(t).wait_recv()
        for i in range(sp):
            total = term(at(t, y, c), i) + sib_in[1, t, i].astype(F32)
            if ny == 2:
                total = total + y_in[t, i].astype(F32)
            fin[i] = total

        @pl.when(jnp.logical_and(t >= z, has_dn))
        def _():
            zcopy(True, t).wait_recv()
            fin[...] += zup_in[t].astype(F32)

        @pl.when(jnp.logical_and(t <= z, has_up))
        def _():
            zcopy(False, t).wait_recv()
            fin[...] += zdn_in[t].astype(F32)

        @pl.when(t > z)
        def _():
            z_out[t] = fin[...].astype(BF)
            zcopy(True, t).start()

        @pl.when(t < z)
        def _():
            z_out[t] = fin[...].astype(BF)
            zcopy(False, t).start()

        @pl.when(t == z)
        def _():
            out_ref[...] = fin[...].astype(BF)
        return 0

    lax.fori_loop(0, nz, to_z, 0)

    def sent_line(slot, up, dn):
        if up is not None:
            @pl.when(up)
            def _():
                tcopy(0, slot).wait_send()
        if dn is not None:
            @pl.when(dn)
            def _():
                tcopy(1, slot).wait_send()
        if ny == 2:
            tcopy(2, slot).wait_send()
        tcopy(3, slot).wait_send()

    sent_line(me, has_up, has_dn)

    def line_sent(z_, from_up):
        sent_line(at(z_, y, c), None if from_up else has_up, has_dn if from_up else None)

    def drain(d, _):
        sides(d, line_sent)
        return 0

    lax.fori_loop(1, nz, drain, 0)

    def drain_t(t, _):
        if ny == 2:
            tcopy(3, at(t, 1 - y, c)).wait_send()
            scopy(0, t).wait_send()
            ycopy(t).wait_send()
        scopy(1, t).wait_send()

        @pl.when(t > z)
        def _():
            zcopy(True, t).wait_send()

        @pl.when(t < z)
        def _():
            zcopy(False, t).wait_send()
        return 0

    lax.fori_loop(0, nz, drain_t, 0)


def body(nz, ny, tokens, gate_blocks, gate_rows, up_blocks, up_rows, down_blocks, down_cols, owner):
    n = nz * ny * 2
    rows, width = tokens.shape
    hbl, keep, blk, _ = gate_blocks.shape
    sp = owner.shape[0]
    ntok = rows * n
    db = width // blk
    half = db // 2
    chips = n // 2
    smem = pl.BlockSpec(memory_space=pltpu.SMEM)
    vmem = pl.BlockSpec(memory_space=pltpu.VMEM)
    hbm = pl.BlockSpec(memory_space=pl.ANY)
    dma = pltpu.SemaphoreType.DMA
    part = (sp, ntok, blk)
    macs = ntok * hbl * keep * blk * blk * 3
    return pl.pallas_call(
        functools.partial(kernel, nz, ny),
        out_shape=jax.ShapeDtypeStruct(part, BF),
        in_specs=[vmem, smem, smem, smem, smem, hbm, hbm, hbm],
        out_specs=vmem,
        scratch_shapes=[
            pltpu.VMEM(gate_blocks.shape, BF),
            pltpu.VMEM(up_blocks.shape, BF),
            pltpu.VMEM(down_blocks.shape, BF),
            pltpu.VMEM((n, half + 1, 2 * rows, blk), BF),
            pltpu.VMEM((db, chips, 2 * rows, blk), BF),
            pltpu.VMEM((hbl, ntok, blk), BF),
            pltpu.VMEM((8, blk), jnp.int32),
            pltpu.SMEM((8, blk), jnp.int32),
            pltpu.VMEM((8, blk), jnp.int32),
            pltpu.SMEM((8, blk), jnp.int32),
            pltpu.VMEM((2, nz) + part, BF),
            pltpu.VMEM((2, nz) + part, BF),
            pltpu.VMEM((nz,) + part, BF),
            pltpu.VMEM((nz,) + part, BF),
            pltpu.VMEM((nz,) + part, BF),
            pltpu.VMEM((nz,) + part, BF),
            pltpu.VMEM((nz,) + part, BF),
            pltpu.VMEM(part, F32),
            dma((2, hbl)), dma(()), dma((2,)), dma((4, n)), dma((n,)),
            dma((2, nz)), dma((2, nz)), dma((nz,)), dma((nz,)),
            dma((nz,)), dma((nz,)), dma((nz,)),
        ],
        compiler_params=pltpu.CompilerParams(
            collective_id=0, has_side_effects=True, vmem_limit_bytes=58 * 1024 * 1024
        ),
        cost_estimate=pl.CostEstimate(
            flops=2 * macs, bytes_accessed=3 * gate_blocks.size * 2, transcendentals=hbl * ntok * blk
        ),
    )(tokens, gate_rows, up_rows, down_cols, owner, gate_blocks, up_blocks, down_blocks)


def line_shape(mesh):
    n = mesh.shape["tp"]
    row = mesh.devices.reshape(-1, n)[0]
    ys = [getattr(d, "coords", (0, 0, 0))[1] for d in row]
    ny = 2 if len(set(ys)) == 2 and n % 4 == 0 else 1
    return n // (2 * ny), ny


def solution(mesh):
    nz, ny = line_shape(mesh)
    in_specs = (
        P(("groups", "tp"), None),
        P("tp", None, None, None),
        P("tp", None),
        P("tp", None, None, None),
        P("tp", None),
        P("tp", None, None, None),
        P("tp", None),
        P("tp"),
    )
    out_specs = P("tp", "groups", None)
    return jax.shard_map(
        functools.partial(body, nz, ny), mesh=mesh, in_specs=in_specs, out_specs=out_specs,
        check_vma=False,
    )
```

time: 234 us -> 51.2 us (0.22)
  matrix products: 71.1 us -> 0 us
  waiting for transfers between devices: 70.7 us -> 0 us
  local copies, waits for them, and re-layouts: 62.4 us -> 1.57 us
  Pallas kernels: 0 us -> 49.5 us
  between operations: 14.1 us -> 0.01 us
  blocking collectives: 13.6 us -> 0 us
    dot_general x6 -> x0, matrix products: 71.1 us -> none  [the longest x2 24.1 us: fill_dense(): jnp.einsum('jkd,jkcf->dcjf', onehot, blocks, preferred_element_type=jnp.f...]
    reduce_scatter x1 -> x0, waiting for transfers between devices: 70 us -> none  [body(): lax.psum_scatter(jnp.einsum('tf,sfc->stc', hidden_flat, dense_down, prefe...]
    pallas_call x0 -> x1, Pallas kernels: none -> 49.5 us  [body(): pl.pallas_call(functools.partial(kernel, nz, ny), out_shape=jax.ShapeDtyp...]
    convert_element_type x3 -> x0, local copies, waits for them, and re-layouts: 38.2 us -> none  [the longest x2 37.4 us: fill_dense(): dense.astype(jnp.bfloat16)]
    dot_general x1 -> x0, local copies, waits for them, and re-layouts: 23 us -> none  [body(): jnp.einsum('jks,jkfc->sjfc', slot_onehot, down_blocks, preferred_element_...]
    unnamed x1 -> x0, blocking collectives: 13.6 us -> none
  transfers between devices with their start and end apart: 2 -> 0, of which waited for: 1 -> 0; matrix products, arithmetic and copies ran while one was open for 43% -> 0% of each run, Pallas kernels for 0% -> 0%
where the time goes in v1:
time: 51.2 us; the launch traced here: 51.1 us
  Pallas kernels  49.5 us (97%)
  local copies, waits for them, and re-layouts  1.57 us (3%)
    pallas_call x1, Pallas kernels, body(): pl.pallas_call(functools.partial(kernel, nz, ny), out_shape=jax.ShapeDtyp...  49.5 us
    unnamed x1, local copies, waits for them, and re-layouts  1.57 us

profile of v1, /device:TPU:0, one launch (start us, length us, event | category | flops | bytes accessed | tf_op | source)
XLA Modules:
  0.0 51.1 jit_solution(14701561018282836584)
XLA Ops:
  0.0 49.5 %shard_map.82 = bf16[4,128,128]{2,1,0:T(8,128)(2,1)} custom-call(bf16[8,8192]{1,0:T(8,128)(2,1)} %tok_ref.1, s32[8,32]{1,0:T(8,128)} %grows.1, s32[8,32]{1,0:T(8,128)} %urows.1, s32[8,32]{1,0:T(8,128)} %dcols.1, s32[4]{0:T(128)} %own_ref.1, bf16[8,32,128,128]{3,2,1,0:T(8,128)(2,1)} %wg_hbm.1, bf16[8,32,128,128]{3,2,1,0:T(8,128)(2,1)} %wu_hbm.1, ...), custom_call_target="tpu_custom_call" | custom-call | flops 3221225472 | bytes 25165824 | tf_op jit(solution)/shard_map/pallas_call | solution.py:401
  49.5 1.6 %copy.10 = bf16[4,128,128]{2,1,0:T(8,128)(2,1)} copy(bf16[4,128,128]{2,1,0:T(8,128)(2,1)} %shard_map.82) | data formatting | bytes 262144

commit v2 on v1

--- a/solution.py
+++ b/solution.py
@@ -50,6 +50,23 @@
 
     down_copy = pltpu.make_async_copy(wd_hbm, wd, wdsem)
 
+    barrier = pltpu.get_barrier_semaphore()
+
+    def hello(dev):
+        pl.semaphore_signal(barrier, inc=1, device_id={"tp": dev}, device_id_type=MESH)
+
+    hello(sib)
+    if ny == 2:
+        hello(ynb)
+
+    @pl.when(has_up)
+    def _():
+        hello(zup)
+
+    @pl.when(has_dn)
+    def _():
+        hello(zdn)
+
     for g in range(half):
         lo = tok_ref[:, 2 * g * blk:(2 * g + 1) * blk].astype(F32)
         hi = tok_ref[:, (2 * g + 1) * blk:(2 * g + 2) * blk].astype(F32)
@@ -59,23 +76,6 @@
     for i in range(sp):
         mine = jnp.where(lane == me * sp + i, own_ref[i], mine)
     buf[me, half] = mine.astype(F32).astype(BF)
-
-    barrier = pltpu.get_barrier_semaphore()
-
-    def hello(dev):
-        pl.semaphore_signal(barrier, inc=1, device_id={"tp": dev}, device_id_type=MESH)
-
-    hello(sib)
-    if ny == 2:
-        hello(ynb)
-
-    @pl.when(has_up)
-    def _():
-        hello(zup)
-
-    @pl.when(has_dn)
-    def _():
-        hello(zdn)
 
     pl.semaphore_wait(barrier, ny + has_up.astype(jnp.int32) + has_dn.astype(jnp.int32))
 

time: 51.2 us -> 51.2 us (level)
  no operation moved by 1% of the time
where the time goes in v2:
time: 51.2 us; the launch traced here: 51.1 us
  Pallas kernels  49.5 us (97%)
  local copies, waits for them, and re-layouts  1.57 us (3%)
    pallas_call x1, Pallas kernels, body(): pl.pallas_call(functools.partial(kernel, nz, ny), out_shape=jax.ShapeDtyp...  49.5 us
    unnamed x1, local copies, waits for them, and re-layouts  1.57 us

profile of v2, /device:TPU:0, one launch (start us, length us, event | category | flops | bytes accessed | tf_op | source)
XLA Modules:
  0.0 51.1 jit_solution(8865184119770507986)
XLA Ops:
  0.0 49.5 %shard_map.82 = bf16[4,128,128]{2,1,0:T(8,128)(2,1)} custom-call(bf16[8,8192]{1,0:T(8,128)(2,1)} %tok_ref.1, s32[8,32]{1,0:T(8,128)} %grows.1, s32[8,32]{1,0:T(8,128)} %urows.1, s32[8,32]{1,0:T(8,128)} %dcols.1, s32[4]{0:T(128)} %own_ref.1, bf16[8,32,128,128]{3,2,1,0:T(8,128)(2,1)} %wg_hbm.1, bf16[8,32,128,128]{3,2,1,0:T(8,128)(2,1)} %wu_hbm.1, ...), custom_call_target="tpu_custom_call" | custom-call | flops 3221225472 | bytes 25165824 | tf_op jit(solution)/shard_map/pallas_call | solution.py:401
  49.5 1.6 %copy.10 = bf16[4,128,128]{2,1,0:T(8,128)(2,1)} copy(bf16[4,128,128]{2,1,0:T(8,128)(2,1)} %shard_map.82) | data formatting | bytes 262144
